TPU v7x, 32 devices: a whole 2x2x4 slice. The times are simulated.
32 devices in a mesh: dp: 4 (over y, x), expert: 8 (over z, core).
Axes of the slice: x: 2, y: 2, z: 4, core: 2. Of those that a mesh axis runs over, the one named last changes fastest.
Arguments:
- tokens: bfloat16 [2560, 7168], P('expert', 'dp'), may hold values from -6 to 6
- route_ids: int32 [2560, 8], P('expert'), may hold values from 0 to 255, as said below
- route_scores: float32 [2560, 8], P('expert'), may hold values from 0.05 to 1
- partner: int32 [8], replicated, may hold values from 0 to 7, as said below
- w_gate: bfloat16 [8, 7168, 1024], P('expert', None, 'dp'), may hold values from -0.0625 to 0.0625
- w_up: bfloat16 [8, 7168, 1024], P('expert', None, 'dp'), may hold values from -0.0625 to 0.0625
- w_down: bfloat16 [8, 1024, 7168], P('expert', 'dp'), may hold values from -0.5 to 0.5
Outputs:
- mixed: bfloat16 [2560, 7168], P('expert', 'dp')
- placed_gate: bfloat16 [8, 7168, 1024], P('expert', None, 'dp')
- placed_up: bfloat16 [8, 7168, 1024], P('expert', None, 'dp')
- placed_down: bfloat16 [8, 1024, 7168], P('expert', 'dp')
Inputs may be any that keep to these rules, and one draw needn't show every extreme that they name: `route_ids`: each token names 8 different experts, exactly one of them below 8. The 320 tokens of one index of expert name each expert below 8 at most 80 times, and one expert below 8 is named exactly 80 times by the tokens of every index. partner[e] is e or e xor 1, and partner[partner[e]] = e.
All inputs are finite; a program needn't handle non-finite values.
Results may differ from a plain program's by a relative error of at most 0.017.
Values may be sent and summed in bfloat16 or wider, within the bound.
A program may use at most 192 MiB of HBM per device.

v0:
```python
import jax
import jax.numpy as jnp
from jax import lax
from jax.sharding import PartitionSpec as P


def swapped_2(value, axis, apart):
    return lax.ppermute(value, axis, [(i, i ^ 1 << apart) for i in range(lax.axis_size(axis))])


def body(tokens, route_ids, route_scores, partner, w_gate, w_up, w_down):
    expert_count = lax.axis_size("expert")
    token_rows = tokens.shape[0]
    capacity = 2 * token_rows // expert_count
    slot_count = expert_count * capacity
    own_index = lax.axis_index("expert")
    in_window = route_ids < expert_count
    expert_pick = jnp.sum(jnp.where(in_window, route_ids, 0), axis=1)
    window_score = jnp.sum(jnp.where(in_window, route_scores, jnp.zeros_like(route_scores)), axis=1)
    gate_weight = 2.5 * window_score / jnp.sum(route_scores, axis=1)
    swapped = swapped_2((w_gate, w_up, w_down), "expert", 0)
    is_moved = partner[own_index] != own_index
    placed_gate = jnp.where(is_moved, swapped[0], w_gate)
    placed_up = jnp.where(is_moved, swapped[1], w_up)
    placed_down = jnp.where(is_moved, swapped[2], w_down)
    target = partner[expert_pick]
    gate_matrix, up_matrix, down_matrix = (placed_gate[0], placed_up[0], placed_down[0])
    columns = jnp.arange(expert_count, dtype=jnp.int32)
    one_hot = (target[:, None] == columns[None, :]).astype(jnp.int32)
    slot_rank = jnp.sum((jnp.cumsum(one_hot, axis=0) - 1) * one_hot, axis=1)
    slot_index = target * capacity + slot_rank
    gathered = lax.all_gather(tokens, "dp", axis=1, tiled=True)
    send_buffer = (
        jnp.zeros((slot_count, gathered.shape[1]), jnp.bfloat16).at[slot_index].set(gathered)
    )
    arrived = lax.all_to_all(
        send_buffer.reshape(expert_count, capacity, gathered.shape[1]),
        "expert",
        split_axis=0,
        concat_axis=0,
        tiled=True,
    )
    flat_rows = arrived.reshape(slot_count, gathered.shape[1])
    gate_proj = jnp.dot(flat_rows, gate_matrix, preferred_element_type=jnp.float32)
    up_proj = jnp.dot(flat_rows, up_matrix, preferred_element_type=jnp.float32)
    hidden = (jax.nn.silu(gate_proj) * up_proj).astype(jnp.bfloat16)
    partial_value = jnp.dot(hidden, down_matrix, preferred_element_type=jnp.float32).astype(
        jnp.bfloat16
    )
    returned = lax.all_to_all(
        partial_value.reshape(expert_count, capacity, partial_value.shape[1]),
        "expert",
        split_axis=0,
        concat_axis=0,
        tiled=True,
    )
    own_rows = returned.reshape(slot_count, partial_value.shape[1])[slot_index].astype(jnp.float32)
    term_rows = gate_weight[:, None] * own_rows
    summed = lax.psum_scatter(term_rows.astype(jnp.bfloat16), "dp", scatter_dimension=1, tiled=True)
    return (summed, placed_gate, placed_up, placed_down)


def solution(mesh):
    return jax.shard_map(
        body,
        mesh=mesh,
        in_specs=(
            P("expert", "dp"),
            P("expert", None),
            P("expert", None),
            P(),
            P("expert", None, "dp"),
            P("expert", None, "dp"),
            P("expert", "dp", None),
        ),
        out_specs=(
            P("expert", "dp"),
            P("expert", None, "dp"),
            P("expert", None, "dp"),
            P("expert", "dp", None),
        ),
        check_vma=False,
    )
```

profile of v0, /device:TPU:0, one launch (start us, length us, event | category | flops | bytes accessed | tf_op | source)
XLA Modules:
  0.0 604.1 jit_solution(16538037646573039553)
XLA Ops:
  7.2 0.7 all-gather.2.cloned.1.call-update
  7.9 0.7 fusion.13
  8.7 1.7 fusion.19
  10.3 4.4 fusion.16
  14.8 0.6 broadcast_select_fusion.3
  15.4 0.9 reduce-window.6
  16.7 51.9 %all-gather.2.cloned.1.call-done = bf16[320,7168]{1,0:T(8,128)(2,1)} async-done(((bf16[320,1792]{1,0:T(8,128)(2,1)}), bf16[320,7168]{1,0:T(8,128)(2,1)}) %all-gather.2.cloned.1.call-update) | async-done | bytes 4587536 | tf_op jit(solution)/shard_map/all_gather | solution.py:32
  68.6 13.4 %scatter_custom_fusion = bf16[640,7168]{1,0:T(8,128)(2,1)} fusion(s32[320]{0:T(512)S(1)} %fusion.17, bf16[320,7168]{1,0:T(8,128)(2,1)} %all-gather.2.cloned.1.call-done, bf16[]{:T(256)} %constant.14.clone.1), kind=kCustom, calls=%fused_computation.4 | custom fusion | bytes 9175552 | tf_op jit(solution)/shard_map/scatter | solution.py:34
  82.0 5.2 all-to-all-start
  87.4 0.4 collective-permute-start
  88.6 6.7 %collective-permute-done.1 = bf16[1,7168,256]{2,1,0:T(8,128)(2,1)} collective-permute-done((bf16[1,7168,256]{2,1,0:T(8,128)(2,1)}, bf16[1,7168,256]{2,1,0:T(8,128)(2,1)}, u32[]{:S(2)}, u32[]{:S(2)}) %collective-permute-start.1) | collective-permute-done | bytes 3670048 | tf_op jit(solution)/shard_map/ppermute | solution.py:8
  95.2 4.3 broadcast_select_fusion.1
  99.5 1.0 collective-permute-done
  100.5 2.2 broadcast_select_fusion.2
  102.7 3.0 collective-permute-done.2
  105.8 2.2 broadcast_select_fusion
  108.0 179.8 %all-to-all-done = bf16[8,80,7168]{2,1,0:T(8,128)(2,1)} async-done(((bf16[8,80,7168]{2,1,0:T(8,128)(2,1)}), bf16[8,80,7168]{2,1,0:T(8,128)(2,1)}, u32[]{:S(2)}, u32[]{:S(2)}) %all-to-all-start) | async-done | bytes 9175072 | tf_op jit(solution)/shard_map/all_to_all | solution.py:36
  287.7 7.2 %fusion.3 = f32[640,256]{1,0:T(8,128)S(1)} fusion(bf16[640,7168]{1,0:T(8,128)(2,1)} %bitcast.12, bf16[1,7168,256]{2,1,0:T(8,128)(2,1)} %broadcast_select_fusion.1), kind=kOutput, calls=%fused_computation.7 | convolution fusion | flops 2348810240 | bytes 13500416 | tf_op jit(solution)/shard_map/dot_general | solution.py:45
  294.9 18.9 %convolution_convert_fusion = bf16[640,7168]{1,0:T(8,128)(2,1)} fusion(bf16[1,256,7168]{2,1,0:T(8,128)(2,1)} %broadcast_select_fusion, f32[640,256]{1,0:T(8,128)S(1)} %fusion.3, bf16[640,7168]{1,0:T(8,128)(2,1)} %bitcast.12, bf16[1,7168,256]{2,1,0:T(8,128)(2,1)} %broadcast_select_fusion.2), kind=kOutput, calls=%fused_computation.2 | convolution fusion | flops 4703191040 | bytes 26345472 | tf_op jit(solution)/shard_map/dot_general | solution.py:47
  313.9 5.1 all-to-all-start.1
  319.4 200.4 %all-to-all-done.1 = bf16[8,80,7168]{2,1,0:T(8,128)(2,1)} async-done(((bf16[8,80,7168]{2,1,0:T(8,128)(2,1)}), bf16[8,80,7168]{2,1,0:T(8,128)(2,1)}, u32[]{:S(2)}, u32[]{:S(2)}) %all-to-all-start.1) | async-done | bytes 9175072 | tf_op jit(solution)/shard_map/all_to_all | solution.py:50
  519.8 17.7 %gather_fusion = bf16[320,7168]{1,0:T(8,128)(2,1)} fusion(bf16[640,7168]{1,0:T(8,128)(2,1)} %bitcast.18, s32[1024]{0:T(1024)S(1)} %pad_clamp_fusion), kind=kCustom, calls=%fused_computation | custom fusion | bytes 9176320 | tf_op jit(solution)/shard_map/gather | solution.py:57
  537.5 5.7 multiply_convert_fusion
  543.2 54.0 %reduce-scatter.2.cloned.1.call-done = bf16[320,1792]{1,0:T(8,128)(2,1)} async-done(((bf16[320,7168]{1,0:T(8,128)(2,1)}), bf16[320,1792]{1,0:T(8,128)(2,1)}) %reduce-scatter.2.cloned.1.call-update) | async-done | bytes 1146896 | tf_op jit(solution)/shard_map/reduce_scatter | solution.py:59
  (25 shorter events, 1.1 us)
Async XLA Ops:
  7.2 61.4 %all-gather.2.cloned.1.call-start = ((), (), s32[]{:S(2)}) async-start(), calls=%async_computation.3 | async-start | bytes 5734400 | tf_op jit(solution)/shard_map/all_gather | solution.py:32
  82.0 205.8 %all-to-all-start = ((bf16[8,80,7168]{2,1,0:T(8,128)(2,1)}), bf16[8,80,7168]{2,1,0:T(8,128)(2,1)}, u32[]{:S(2)}, u32[]{:S(2)}) async-start(bf16[8,80,7168]{2,1,0:T(8,128)(2,1)} %bitcast.36), calls=%async_computation | async-start | bytes 18350080 | tf_op jit(solution)/shard_map/all_to_all | solution.py:36
  87.2 8.1 %collective-permute-start.1 = (bf16[1,7168,256]{2,1,0:T(8,128)(2,1)}, bf16[1,7168,256]{2,1,0:T(8,128)(2,1)}, u32[]{:S(2)}, u32[]{:S(2)}) collective-permute-start(bf16[1,7168,256]{2,1,0:T(8,128)(2,1)} %param.12), channel_id=1, source_target_pairs={{0,1},{1,0},{2,3},{3,2},{4,5},{5,4},{6,7},{7,6},{8,9},{9,8},{10,11... | collective-permute-start | bytes 11010056 | tf_op jit(solution)/shard_map/ppermute | solution.py:8
  87.4 13.1 %collective-permute-start = (bf16[1,7168,256]{2,1,0:T(8,128)(2,1)}, bf16[1,7168,256]{2,1,0:T(8,128)(2,1)}, u32[]{:S(2)}, u32[]{:S(2)}) collective-permute-start(bf16[1,7168,256]{2,1,0:T(8,128)(2,1)} %param.11), channel_id=1, source_target_pairs={{0,1},{1,0},{2,3},{3,2},{4,5},{5,4},{6,7},{7,6},{8,9},{9,8},{10,11... | collective-permute-start | bytes 11010056 | tf_op jit(solution)/shard_map/ppermute | solution.py:8
  87.7 18.0 %collective-permute-start.2 = (bf16[1,256,7168]{2,1,0:T(8,128)(2,1)}, bf16[1,256,7168]{2,1,0:T(8,128)(2,1)}, u32[]{:S(2)}, u32[]{:S(2)}) collective-permute-start(bf16[1,256,7168]{2,1,0:T(8,128)(2,1)} %param.13), channel_id=1, source_target_pairs={{0,1},{1,0},{2,3},{3,2},{4,5},{5,4},{6,7},{7,6},{8,9},{9,8},{10,11... | collective-permute-start | bytes 11010056 | tf_op jit(solution)/shard_map/ppermute | solution.py:8
  88.6 11.9 %copy-start = (bf16[1,7168,256]{2,1,0:T(8,128)(2,1)S(1)}, bf16[1,7168,256]{2,1,0:T(8,128)(2,1)}, u32[]{:S(2)}) copy-start(bf16[1,7168,256]{2,1,0:T(8,128)(2,1)} %param.11) | copy-start | bytes 11010052
  99.5 6.2 %copy-start.1 = (bf16[1,256,7168]{2,1,0:T(8,128)(2,1)S(1)}, bf16[1,256,7168]{2,1,0:T(8,128)(2,1)}, u32[]{:S(2)}) copy-start(bf16[1,256,7168]{2,1,0:T(8,128)(2,1)} %param.13) | copy-start | bytes 11010052
  313.9 5.4 copy-start.2
  313.9 5.5 copy-start.3
  313.9 205.9 %all-to-all-start.1 = ((bf16[8,80,7168]{2,1,0:T(8,128)(2,1)}), bf16[8,80,7168]{2,1,0:T(8,128)(2,1)}, u32[]{:S(2)}, u32[]{:S(2)}) async-start(bf16[8,80,7168]{2,1,0:T(8,128)(2,1)} %bitcast.35), calls=%async_computation.1 | async-start | bytes 18350080 | tf_op jit(solution)/shard_map/all_to_all | solution.py:50
  319.0 278.2 %reduce-scatter.2.cloned.1.call-start = ((), (), s32[]{:S(2)}) async-start(), calls=%async_computation.4 | async-start | bytes 5734400 | tf_op jit(solution)/shard_map/reduce_scatter | solution.py:59
Sparse Core Ops, SparseCore 0:
  9.8 58.6 all-gather.1
  543.4 53.8 reduce-scatter.1
where the time goes:
time: 605 us; the launch traced here: 604 us
  waiting for transfers between devices  497 us (82%)
  local copies, waits for them, and re-layouts  33.1 us (5%)
  matrix products  26.1 us (4%)
  other arithmetic  21.3 us (4%)
  between operations  14.8 us (2%)
  starting transfers between devices  11.4 us (2%)
    all_to_all x1, waiting for transfers between devices, body(): lax.all_to_all(partial_value.reshape(expert_count, capacity, partial_valu...  200 us
    all_to_all x1, waiting for transfers between devices, body(): lax.all_to_all(send_buffer.reshape(expert_count, capacity, gathered.shape...  180 us
    reduce_scatter x1, waiting for transfers between devices, body(): lax.psum_scatter(term_rows.astype(jnp.bfloat16), 'dp', scatter_dimension=...  54 us
    all_gather x1, waiting for transfers between devices, body(): gathered = lax.all_gather(tokens, 'dp', axis=1, tiled=True)  51.9 us
    dot_general x1, matrix products, body(): jnp.dot(hidden, down_matrix, preferred_element_type=jnp.float32)  18.9 us
    gather x1, local copies, waits for them, and re-layouts, body(): returned.reshape(slot_count, partial_value.shape[1])[slot_index]  17.7 us
    scatter x1, local copies, waits for them, and re-layouts, body(): jnp.zeros((slot_count, gathered.shape[1]), jnp.bfloat16).at[slot_index]  13.4 us
  transfers between devices with their start and end apart: 7, of which 7 were waited for; matrix products, arithmetic and copies ran while one was open for 3% of the time, Pallas kernels for 0%

commit v1 on v0

v1 whole, which is shorter than its diff:
```python
import functools

import jax
import jax.numpy as jnp
from jax import lax
from jax.experimental import pallas as pl
from jax.experimental.pallas import tpu as pltpu
from jax.sharding import PartitionSpec as P

MESH = pl.DeviceIdType.MESH
F32 = jnp.float32
BF16 = jnp.bfloat16


def xor(a, b, n):
    total, bit = 0, 1
    while bit < n:
        x, y = (a // bit) % 2, (b // bit) % 2
        total = total + bit * (x + y - 2 * x * y)
        bit *= 2
    return total


def dot(a, b):
    return jnp.dot(a, b, preferred_element_type=F32)


def kernel(
    E, cap, cap_pad, R,
    tokens, ids, scores, w_gate, w_up, w_down,
    mixed, sw_gate, sw_up, sw_down,
    send, tok, wgu, wd, hid, outb, ret, onehot_t, slot_row,
    w_sem, swap_send, swap_recv, wd_send, wd_recv,
    z_send, z_recv, b_send, b_recv, a_send, a_recv, f_send, f_recv, h_send, h_recv,
):
    q = lax.axis_index("dp")
    s = lax.axis_index("expert")
    qx = q + 1 - 2 * (q % 2)
    qy = (q + 2) % 4
    qd = 3 - q
    peers = (qx, qy, qd)
    T, F = tokens.shape
    H = w_gate.shape[2]
    half = (F // 256) * 128

    barrier = pltpu.get_barrier_semaphore()
    for p in peers:
        pl.semaphore_signal(barrier, inc=1, device_id=(p, s), device_id_type=MESH)

    def greet(j, _):
        pl.semaphore_signal(barrier, inc=1, device_id=(q, (s + j) % E), device_id_type=MESH)
        return 0

    lax.fori_loop(1, E, greet, 0)

    own_copies = [
        pltpu.make_async_copy(w_gate.at[0], wgu.at[:, pl.ds(0, H)], w_sem.at[0]),
        pltpu.make_async_copy(w_up.at[0], wgu.at[:, pl.ds(H, H)], w_sem.at[1]),
        pltpu.make_async_copy(
            w_down.at[0, :, pl.ds(pl.multiple_of(q * F, 128), F)], wd.at[q], w_sem.at[2]
        ),
    ]
    for c in own_copies:
        c.start()

    picks = jnp.sum(jnp.where(ids[...] < E, ids[...], 0), axis=1, keepdims=True)
    one_hot = jnp.where(
        picks == lax.broadcasted_iota(jnp.int32, (T, 128), 1), 1.0, 0.0
    ).astype(BF16)
    rows_e = max(E, 16)
    eye = jnp.where(
        lax.broadcasted_iota(jnp.int32, (rows_e, 128), 0)
        == lax.broadcasted_iota(jnp.int32, (rows_e, 128), 1), 1.0, 0.0
    ).astype(BF16)
    hot_t = lax.dot_general(
        eye, one_hot, (((1,), (1,)), ((), ())), preferred_element_type=F32
    )
    before = jnp.where(
        lax.broadcasted_iota(jnp.int32, (T, T), 0) < lax.broadcasted_iota(jnp.int32, (T, T), 1),
        1.0, 0.0,
    ).astype(BF16)
    rank_t = dot(hot_t.astype(BF16), before)
    number = lax.broadcasted_iota(jnp.int32, (rows_e, T), 0).astype(F32)
    slot_row[...] = jnp.sum(hot_t * (rank_t + number * cap_pad), axis=0, keepdims=True)
    after = jnp.where(
        lax.broadcasted_iota(jnp.int32, (T, T), 1) < lax.broadcasted_iota(jnp.int32, (T, T), 0),
        1.0, 0.0,
    ).astype(BF16)
    rank_c = jnp.sum(dot(after, one_hot) * one_hot.astype(F32), axis=1, keepdims=True)
    slot_col = rank_c + picks.astype(F32) * cap_pad
    onehot_t[...] = jnp.where(
        slot_col == lax.broadcasted_iota(jnp.int32, (T, E * cap_pad), 1).astype(F32), 1.0, 0.0
    ).astype(BF16)

    def pack(e):
        want = lax.broadcasted_iota(jnp.int32, (cap_pad, T), 0).astype(F32) + (
            e * cap_pad
        ).astype(F32)
        return dot(jnp.where(slot_row[...] == want, 1.0, 0.0).astype(BF16), tokens[...]).astype(BF16)

    pl.semaphore_wait(barrier, E + 2)

    def wd_copy(i):
        p = peers[i]
        return pltpu.make_async_remote_copy(
            w_down.at[0, :, pl.ds(pl.multiple_of(p * F, 128), F)], wd.at[q],
            wd_send.at[i], wd_recv.at[i], device_id=(p, s), device_id_type=MESH,
        )

    def swap_copy(i):
        src, dst = ((w_gate, sw_gate), (w_up, sw_up), (w_down, sw_down))[i]
        return pltpu.make_async_remote_copy(
            src, dst, swap_send.at[i], swap_recv.at[i],
            device_id=(q, s + 1 - 2 * (s % 2)), device_id_type=MESH,
        )

    def peer_of(j):
        return xor(s, (E - j) % E, E)

    def z_copy(j):
        return pltpu.make_async_remote_copy(
            send.at[j], tok.at[j, q], z_send.at[j], z_recv.at[j],
            device_id=(q, peer_of(j)), device_id_type=MESH,
        )

    def back_copy(j):
        return pltpu.make_async_remote_copy(
            outb.at[j], ret.at[pl.ds(pl.multiple_of(s * cap_pad, 16), cap_pad), :],
            b_send.at[j], b_recv.at[j],
            device_id=(q, peer_of(j)), device_id_type=MESH,
        )

    def a_copy(j, i):
        return pltpu.make_async_remote_copy(
            tok.at[j, q], tok.at[j, q], a_send.at[i, j % R], a_recv.at[i, j % R],
            device_id=(peers[i], s), device_id_type=MESH,
        )

    def f_copy(j, i):
        ref = tok.at[j, peers[1 - i], :, pl.ds(half, F - half) if i == 0 else pl.ds(0, half)]
        return pltpu.make_async_remote_copy(
            ref, ref, f_send.at[i, j % R], f_recv.at[i, j % R],
            device_id=(peers[i], s), device_id_type=MESH,
        )

    def h_copy(j, i):
        return pltpu.make_async_remote_copy(
            hid.at[j, q], hid.at[j, q], h_send.at[i, j % R], h_recv.at[i, j % R],
            device_id=(peers[i], s), device_id_type=MESH,
        )

    for i in range(3):
        wd_copy(i).start()

    def dispatch(j, _):
        send[j] = pack(peer_of(j))
        z_copy(j).start()
        return 0

    lax.fori_loop(1, E, dispatch, 0)
    tok[0, q] = pack(s)
    for i in range(3):
        swap_copy(i).start()
    for c in own_copies:
        c.wait()

    def step(t, _):
        @pl.when(t < E)
        def _():
            j = t

            @pl.when(j > 0)
            def _():
                z_copy(j).wait_recv()

            for i in range(2):
                a_copy(j, i).start()

        @pl.when((t >= 1) & (t < E + 1))
        def _():
            j = t - 1
            for i in range(2):
                a_copy(j, i).wait_recv()
            for i in range(2):
                f_copy(j, i).start()

        @pl.when((t >= 2) & (t < E + 2))
        def _():
            j = t - 2
            for i in range(2):
                f_copy(j, i).wait_recv()
            both = dot(tok[j, 0], wgu[0:F, :])
            for p in range(1, 4):
                both = both + dot(tok[j, p], wgu[p * F:(p + 1) * F, :])
            gate, up = both[:, :H], both[:, H:]
            hid[j, q] = (gate / (1.0 + jnp.exp(-gate)) * up).astype(BF16)
            for i in range(3):
                h_copy(j, i).start()

        @pl.when(t == 3)
        def _():
            for i in range(3):
                wd_copy(i).wait_recv()

        @pl.when(t >= 3)
        def _():
            j = t - 3
            for i in range(3):
                h_copy(j, i).wait_recv()

            def down(store):
                for n in range(0, F, 256):
                    acc = dot(hid[j, 0], wd[0, :, n:n + 256])
                    for p in range(1, 4):
                        acc = acc + dot(hid[j, p], wd[p, :, n:n + 256])
                    store(n, acc.astype(BF16))

            @pl.when(j == 0)
            def _():
                def store(n, v):
                    ret[pl.ds(pl.multiple_of(s * cap_pad, 16), cap_pad), n:n + 256] = v
                down(store)

            @pl.when(j > 0)
            def _():
                def store(n, v):
                    outb[j, :, n:n + 256] = v
                down(store)
                back_copy(j).start()

            for i in range(2):
                a_copy(j, i).wait_send()
                f_copy(j, i).wait_send()
            for i in range(3):
                h_copy(j, i).wait_send()

        return 0

    lax.fori_loop(0, E + 3, step, 0)

    def finish(j, _):
        z_copy(j).wait_send()
        back_copy(j).wait()
        return 0

    lax.fori_loop(1, E, finish, 0)

    inside = ids[...] < E
    weight = 2.5 * jnp.sum(jnp.where(inside, scores[...], 0.0), axis=1, keepdims=True) / jnp.sum(
        scores[...], axis=1, keepdims=True
    )
    for n in range(0, F, 256):
        mixed[:, n:n + 256] = (weight * dot(onehot_t[...], ret[:, n:n + 256])).astype(BF16)
    for i in range(3):
        wd_copy(i).wait_send()
        swap_copy(i).wait()


def body(tokens, route_ids, route_scores, partner, w_gate, w_up, w_down):
    E = lax.axis_size("expert")
    T, F = tokens.shape
    H = w_gate.shape[2]
    cap = 2 * T // E
    cap_pad = -(-cap // 16) * 16
    R = min(E, 8)
    own = lax.axis_index("expert")
    vmem = pl.BlockSpec(memory_space=pltpu.VMEM)
    hbm = pl.BlockSpec(memory_space=pl.ANY)
    dma = pltpu.SemaphoreType.DMA
    summed, sw_gate, sw_up, sw_down = pl.pallas_call(
        functools.partial(kernel, E, cap, cap_pad, R),
        out_shape=[
            jax.ShapeDtypeStruct((T, F), BF16),
            jax.ShapeDtypeStruct(w_gate.shape, BF16),
            jax.ShapeDtypeStruct(w_up.shape, BF16),
            jax.ShapeDtypeStruct(w_down.shape, BF16),
        ],
        in_specs=[vmem, vmem, vmem, hbm, hbm, hbm],
        out_specs=[vmem, hbm, hbm, hbm],
        scratch_shapes=[
            pltpu.VMEM((E, cap_pad, F), BF16),
            pltpu.VMEM((E, 4, cap_pad, F), BF16),
            pltpu.VMEM((4 * F, 2 * H), BF16),
            pltpu.VMEM((4, H, F), BF16),
            pltpu.VMEM((E, 4, cap_pad, H), BF16),
            pltpu.VMEM((E, cap_pad, F), BF16),
            pltpu.VMEM((E * cap_pad, F), BF16),
            pltpu.VMEM((T, E * cap_pad), BF16),
            pltpu.VMEM((1, T), F32),
            dma((3,)), dma((3,)), dma((3,)), dma((3,)), dma((3,)),
            dma((E,)), dma((E,)), dma((E,)), dma((E,)),
            dma((2, R)), dma((2, R)), dma((2, R)), dma((2, R)), dma((3, R)), dma((3, R)),
        ],
        compiler_params=pltpu.CompilerParams(
            collective_id=0, has_side_effects=True, vmem_limit_bytes=56 * 2**20
        ),
    )(tokens, route_ids, route_scores, w_gate, w_up, w_down)
    moved = partner[own] != own
    return (
        summed,
        jnp.where(moved, sw_gate, w_gate),
        jnp.where(moved, sw_up, w_up),
        jnp.where(moved, sw_down, w_down),
    )


def solution(mesh):
    return jax.shard_map(
        body,
        mesh=mesh,
        in_specs=(
            P("expert", "dp"),
            P("expert", None),
            P("expert", None),
            P(),
            P("expert", None, "dp"),
            P("expert", None, "dp"),
            P("expert", "dp", None),
        ),
        out_specs=(
            P("expert", "dp"),
            P("expert", None, "dp"),
            P("expert", None, "dp"),
            P("expert", "dp", None),
        ),
        check_vma=False,
    )
```

time: 605 us -> 171 us (0.28)
  waiting for transfers between devices: 497 us -> 0 us
  Pallas kernels: 0 us -> 153 us
  local copies, waits for them, and re-layouts: 33.1 us -> 5.27 us
  matrix products: 26.1 us -> 0 us
  between operations: 14.8 us -> 1.31 us
  starting transfers between devices: 11.4 us -> 0 us
  other arithmetic: 21.3 us -> 10.8 us
    all_to_all x2 -> x0, waiting for transfers between devices: 380 us -> none  [the longest x1 200 us: body(): lax.all_to_all(partial_value.reshape(expert_count, capacity, partial_valu...]
    pallas_call x0 -> x1, Pallas kernels: none -> 153 us  [body(): pl.pallas_call(functools.partial(kernel, E, cap, cap_pad, R), out_shape=[...]
    reduce_scatter x1 -> x0, waiting for transfers between devices: 54 us -> none  [body(): lax.psum_scatter(term_rows.astype(jnp.bfloat16), 'dp', scatter_dimension=...]
    all_gather x1 -> x0, waiting for transfers between devices: 51.9 us -> none  [body(): gathered = lax.all_gather(tokens, 'dp', axis=1, tiled=True)]
    dot_general x2 -> x0, matrix products: 26.1 us -> none  [the longest x1 18.9 us: body(): jnp.dot(hidden, down_matrix, preferred_element_type=jnp.float32)]
    gather x2 -> x0, local copies, waits for them, and re-layouts: 19.4 us -> none  [the longest x1 17.7 us: body(): returned.reshape(slot_count, partial_value.shape[1])[slot_index]]
    scatter x1 -> x0, local copies, waits for them, and re-layouts: 13.4 us -> none  [body(): jnp.zeros((slot_count, gathered.shape[1]), jnp.bfloat16).at[slot_index]]
    ppermute x3 -> x0, waiting for transfers between devices: 10.7 us -> none  [swapped_2(): lax.ppermute(value, axis, [(i, i ^ 1 << apart) for i in range(lax.axis_si...]
  transfers between devices with their start and end apart: 7 -> 0, of which waited for: 7 -> 0; matrix products, arithmetic and copies ran while one was open for 3% -> 0% of each run, Pallas kernels for 0% -> 0%
where the time goes in v1:
time: 171 us; the launch traced here: 170 us
  Pallas kernels  153 us (89%)
  other arithmetic  10.8 us (6%)
  local copies, waits for them, and re-layouts  5.27 us (3%)
    pallas_call x1, Pallas kernels, body(): pl.pallas_call(functools.partial(kernel, E, cap, cap_pad, R), out_shape=[...  153 us
    select_n x1, other arithmetic, body(): jnp.where(moved, sw_up, w_up)  6.36 us
    select_n x1, other arithmetic, body(): jnp.where(moved, sw_down, w_down)  4.42 us
    unnamed x7, local copies, waits for them, and re-layouts  4.03 us

profile of v1, /device:TPU:0, one launch (start us, length us, event | category | flops | bytes accessed | tf_op | source)
XLA Modules:
  0.0 170.2 jit_solution(11359020780267737507)
XLA Ops:
  0.6 1.2 dynamic_slice.3
  2.5 1.5 copy.11.ids
  4.0 1.5 copy.12.scores
  5.5 152.9 %shard_map.102 = (bf16[320,1792]{1,0:T(8,128)(2,1)}, bf16[1,7168,256]{2,1,0:T(8,128)(2,1)}, bf16[1,7168,256]{2,1,0:T(8,128)(2,1)}, bf16[1,256,7168]{2,1,0:T(8,128)(2,1)}) custom-call(bf16[320,1792]{1,0:T(8,128)(2,1)} %tokens.1, s32[320,8]{1,0:T(8,128)} %copy.11.ids, f32[320,8]{1,0:T(8,128)} %copy.12.scores, bf16[1,7168,256]{2,1,0:T(8,128)(2,1)} %w_gate.1, ...), custom_call_target="tpu_custom_call" | custom-call | tf_op jit(solution)/shard_map/pallas_call | solution.py:270
  158.4 0.0 copy-start
  158.5 4.4 %broadcast_select_fusion = bf16[1,256,7168]{2,1,0:T(8,128)(2,1)} fusion(bf16[1,256,7168]{2,1,0:T(8,128)(2,1)} %get-tuple-element.11, bf16[1,256,7168]{2,1,0:T(8,128)(2,1)} %w_down.1, pred[]{:T(512)S(6)} %ne.3), kind=kLoop, calls=%fused_computation | loop fusion | flops 1835008 | bytes 11010049 | tf_op jit(solution)/shard_map/jit(_where)/select_n | solution.py:303
  162.9 0.0 copy-done
  162.9 0.0 copy-start.1
  162.9 6.4 %broadcast_select_fusion.1 = (bf16[1,7168,256]{2,1,0:T(8,128)(2,1)}, bf16[1,7168,256]{2,1,0:T(8,128)(2,1)}) fusion(bf16[1,7168,256]{2,1,0:T(8,128)(2,1)} %get-tuple-element.10, bf16[1,7168,256]{2,1,0:T(8,128)(2,1)} %w_up.1, pred[]{:T(512)S(6)} %ne.3, bf16[1,7168,256]{2,1,0:T(8,128)(2,1)} %get-tuple-element.9, bf16[1,7168,256]{2,1,0:T(8,128)(2,1)S(1)} %copy-done), kind=kLoop, calls=%fused_computation.1 | loop fusion | flops 3670016 | bytes 22020096 | tf_op jit(solution)/shard_map/jit(_where)/select_n | solution.py:302
  169.2 0.0 copy-done.1
  169.2 1.0 copy.14
Async XLA Ops:
  158.4 4.4 %copy-start = (bf16[1,7168,256]{2,1,0:T(8,128)(2,1)S(1)}, bf16[1,7168,256]{2,1,0:T(8,128)(2,1)}, u32[]{:S(2)}) copy-start(bf16[1,7168,256]{2,1,0:T(8,128)(2,1)} %w_gate.1) | copy-start | bytes 11010052
  162.9 6.4 %copy-start.1 = (bf16[320,1792]{1,0:T(8,128)(2,1)S(1)}, bf16[320,1792]{1,0:T(8,128)(2,1)}, u32[]{:S(2)}) copy-start(bf16[320,1792]{1,0:T(8,128)(2,1)} %get-tuple-element.18) | copy-start | bytes 3440644

commit v2 on v1

v2 whole, which is shorter than its diff:
```python
import functools

import jax
import jax.numpy as jnp
from jax import lax
from jax.experimental import pallas as pl
from jax.experimental.pallas import tpu as pltpu
from jax.sharding import PartitionSpec as P

MESH = pl.DeviceIdType.MESH
F32 = jnp.float32
BF16 = jnp.bfloat16


def xor(a, b, n):
    total, bit = 0, 1
    while bit < n:
        x, y = (a // bit) % 2, (b // bit) % 2
        total = total + bit * (x + y - 2 * x * y)
        bit *= 2
    return total


def dot(a, b):
    return jnp.dot(a, b, preferred_element_type=F32)


def kernel(
    E, cap_pad, R,
    tokens_hbm, ids, scores, w_gate, w_up, w_down,
    mixed, sw_gate, sw_up, sw_down,
    tokens, send, tok, wgu, wd, hid, outb, ret, onehot_t, slot_row, weight, acc,
    t_sem, w_sem, swap_send, swap_recv, wd_send, wd_recv,
    z_send, z_recv, b_send, b_recv, a_send, a_recv, f_send, f_recv, h_send, h_recv,
):
    q = lax.axis_index("dp")
    s = lax.axis_index("expert")
    qx = q + 1 - 2 * (q % 2)
    qy = (q + 2) % 4
    qd = 3 - q
    peers = (qx, qy, qd)
    T, F = tokens.shape
    H = w_gate.shape[2]
    half = (F // 256) * 128

    barrier = pltpu.get_barrier_semaphore()
    for p in peers:
        pl.semaphore_signal(barrier, inc=1, device_id=(p, s), device_id_type=MESH)

    def greet(j, _):
        pl.semaphore_signal(barrier, inc=1, device_id=(q, (s + j) % E), device_id_type=MESH)
        return 0

    lax.fori_loop(1, E, greet, 0)

    tokens_copy = pltpu.make_async_copy(tokens_hbm, tokens, t_sem.at[0])
    tokens_copy.start()

    def wd_copy(i):
        p = peers[i]
        return pltpu.make_async_remote_copy(
            w_down.at[0, :, pl.ds(pl.multiple_of(p * F, 128), F)], wd.at[q],
            wd_send.at[i], wd_recv.at[i], device_id=(p, s), device_id_type=MESH,
        )

    def swap_copy(i):
        src, dst = ((w_gate, sw_gate), (w_up, sw_up), (w_down, sw_down))[i]
        return pltpu.make_async_remote_copy(
            src, dst, swap_send.at[i], swap_recv.at[i],
            device_id=(q, s + 1 - 2 * (s % 2)), device_id_type=MESH,
        )

    def peer_of(j):
        return xor(s, (E - j) % E, E)

    def z_copy(j):
        return pltpu.make_async_remote_copy(
            send.at[j], tok.at[j, q], z_send.at[j], z_recv.at[j],
            device_id=(q, peer_of(j)), device_id_type=MESH,
        )

    def back_copy(j):
        return pltpu.make_async_remote_copy(
            outb.at[j], ret.at[pl.ds(pl.multiple_of(s * cap_pad, 16), cap_pad), :],
            b_send.at[j], b_recv.at[j],
            device_id=(q, peer_of(j)), device_id_type=MESH,
        )

    def a_copy(j, i):
        return pltpu.make_async_remote_copy(
            tok.at[j, q], tok.at[j, q], a_send.at[i, j % R], a_recv.at[i, j % R],
            device_id=(peers[i], s), device_id_type=MESH,
        )

    def f_copy(j, i):
        ref = tok.at[j, peers[1 - i], :, pl.ds(half, F - half) if i == 0 else pl.ds(0, half)]
        return pltpu.make_async_remote_copy(
            ref, ref, f_send.at[i, j % R], f_recv.at[i, j % R],
            device_id=(peers[i], s), device_id_type=MESH,
        )

    def h_copy(j, i):
        return pltpu.make_async_remote_copy(
            hid.at[j, q], hid.at[j, q], h_send.at[i, j % R], h_recv.at[i, j % R],
            device_id=(peers[i], s), device_id_type=MESH,
        )

    own_copies = [
        pltpu.make_async_copy(
            w_down.at[0, :, pl.ds(pl.multiple_of(q * F, 128), F)], wd.at[q], w_sem.at[8]
        )
    ]
    for p in range(4):
        for i, w in enumerate((w_gate, w_up)):
            own_copies.append(pltpu.make_async_copy(
                w.at[0, pl.ds(p * F, F), :], wgu.at[p, :, pl.ds(i * H, H)], w_sem.at[2 * p + i]
            ))

    pl.semaphore_wait(barrier, E + 2)
    for i in range(3):
        wd_copy(i).start()

    inside = ids[...] < E
    picks = jnp.sum(jnp.where(inside, ids[...], 0), axis=0, keepdims=True)
    rows_e = max(E, 16)
    number = lax.broadcasted_iota(jnp.int32, (rows_e, T), 0)
    hot = jnp.where(picks == number, 1.0, 0.0)
    row_of = lax.broadcasted_iota(jnp.int32, (T, T), 0)
    col_of = lax.broadcasted_iota(jnp.int32, (T, T), 1)
    before = jnp.where(row_of < col_of, 1.0, 0.0).astype(BF16)
    rank = jnp.sum(hot * dot(hot.astype(BF16), before), axis=0, keepdims=True)
    picks_f = picks.astype(F32)
    slot_row[...] = picks_f * cap_pad + rank

    def pack(e):
        want = lax.broadcasted_iota(jnp.int32, (cap_pad, T), 0).astype(F32) + (
            e * cap_pad
        ).astype(F32)
        return dot(jnp.where(slot_row[...] == want, 1.0, 0.0).astype(BF16), tokens[...]).astype(BF16)

    tokens_copy.wait()

    def dispatch(j, _):
        send[j] = pack(peer_of(j))
        z_copy(j).start()
        return 0

    lax.fori_loop(1, E, dispatch, 0)
    tok[0, q] = pack(s)
    for i in range(2):
        a_copy(0, i).start()
    for c in own_copies:
        c.start()
    for i in range(3):
        swap_copy(i).start()

    gate_weight = 2.5 * jnp.sum(jnp.where(inside, scores[...], 0.0), axis=0, keepdims=True) / jnp.sum(
        scores[...], axis=0, keepdims=True
    )
    high = gate_weight.astype(BF16).astype(F32)
    middle = (gate_weight - high).astype(BF16).astype(F32)
    low = gate_weight - high - middle
    line = lax.broadcasted_iota(jnp.int32, (16, T), 0)
    stack = jnp.zeros((16, T), F32)
    for i, v in enumerate((picks_f, rank, high, middle, low)):
        stack = jnp.where(line == i, v, stack)
    eye = jnp.where(row_of == col_of, 1.0, 0.0).astype(BF16)
    turned = lax.dot_general(
        eye, stack.astype(BF16), (((1,), (1,)), ((), ())), preferred_element_type=F32
    )
    slot_col = turned[:, 0:1] * cap_pad + turned[:, 1:2]
    weight[...] = jnp.broadcast_to(turned[:, 2:3] + turned[:, 3:4] + turned[:, 4:5], weight.shape)
    onehot_t[...] = jnp.where(
        slot_col == lax.broadcasted_iota(jnp.int32, (T, E * cap_pad), 1).astype(F32), 1.0, 0.0
    ).astype(BF16)

    z_copy(1).wait_recv()
    for i in range(2):
        a_copy(1, i).start()
    for c in own_copies:
        c.wait()

    def step(t, _):
        @pl.when(t < E)
        def _():
            for i in range(2):
                a_copy(t, i).wait_recv()
            for i in range(2):
                f_copy(t, i).start()

        @pl.when(t + 2 < E)
        def _():
            z_copy(t + 2).wait_recv()
            for i in range(2):
                a_copy(t + 2, i).start()

        @pl.when(t < E)
        def _():
            acc[...] = (
                dot(tok[t, q], wgu[q]) + dot(tok[t, qx], wgu[qx]) + dot(tok[t, qy], wgu[qy])
            )

        @pl.when(t == 1)
        def _():
            for i in range(3):
                wd_copy(i).wait_recv()

        @pl.when(t >= 1)
        def _():
            j = t - 1
            for i in range(3):
                h_copy(j, i).wait_recv()

            def down(store):
                for n in range(0, F, 256):
                    out = dot(hid[j, 0], wd[0, :, n:n + 256])
                    for p in range(1, 4):
                        out = out + dot(hid[j, p], wd[p, :, n:n + 256])
                    store(n, out.astype(BF16))

            @pl.when(j == 0)
            def _():
                def store(n, v):
                    ret[pl.ds(pl.multiple_of(s * cap_pad, 16), cap_pad), n:n + 256] = v
                down(store)

            @pl.when(j > 0)
            def _():
                def store(n, v):
                    outb[j, :, n:n + 256] = v
                down(store)
                back_copy(j).start()

            for i in range(2):
                a_copy(j, i).wait_send()
                f_copy(j, i).wait_send()
            for i in range(3):
                h_copy(j, i).wait_send()

        @pl.when(t < E)
        def _():
            for i in range(2):
                f_copy(t, i).wait_recv()
            both = acc[...] + dot(tok[t, qd], wgu[qd])
            gate, up = both[:, :H], both[:, H:]
            hid[t, q] = (gate / (1.0 + jnp.exp(-gate)) * up).astype(BF16)
            for i in range(3):
                h_copy(t, i).start()

        return 0

    lax.fori_loop(0, E + 1, step, 0)

    def finish(j, _):
        z_copy(j).wait_send()
        back_copy(j).wait()
        return 0

    lax.fori_loop(1, E, finish, 0)
    for n in range(0, F, 256):
        mixed[:, n:n + 256] = (weight[:, :1] * dot(onehot_t[...], ret[:, n:n + 256])).astype(BF16)
    for i in range(3):
        wd_copy(i).wait_send()
        swap_copy(i).wait()


PIECES = 4


def place_kernel(partner, *refs):
    sources, targets, sem = (refs[0:3], refs[3:6]), refs[6:9], refs[9]
    own = lax.axis_index("expert")
    moved = partner[own] != own

    def pieces(group):
        for i in range(3):
            rows = group[i].shape[1] // PIECES
            for n in range(PIECES):
                cut = (0, pl.ds(n * rows, rows))
                yield pltpu.make_async_copy(
                    group[i].at[cut], targets[i].at[cut], sem.at[i * PIECES + n]
                )

    @pl.when(moved)
    def _():
        for c in pieces(sources[1]):
            c.start()

    @pl.when(jnp.logical_not(moved))
    def _():
        for c in pieces(sources[0]):
            c.start()

    for c in pieces(sources[0]):
        c.wait()


def body(tokens, route_ids, route_scores, partner, w_gate, w_up, w_down):
    E = lax.axis_size("expert")
    T, F = tokens.shape
    H = w_gate.shape[2]
    cap = 2 * T // E
    cap_pad = -(-cap // 16) * 16
    R = min(E, 8)
    vmem = pl.BlockSpec(memory_space=pltpu.VMEM)
    hbm = pl.BlockSpec(memory_space=pl.ANY)
    dma = pltpu.SemaphoreType.DMA
    weights = (w_gate, w_up, w_down)
    weight_shapes = [jax.ShapeDtypeStruct(w.shape, BF16) for w in weights]
    summed, *swapped = pl.pallas_call(
        functools.partial(kernel, E, cap_pad, R),
        out_shape=[jax.ShapeDtypeStruct((T, F), BF16)] + weight_shapes,
        in_specs=[hbm, vmem, vmem, hbm, hbm, hbm],
        out_specs=[vmem, hbm, hbm, hbm],
        scratch_shapes=[
            pltpu.VMEM((T, F), BF16),
            pltpu.VMEM((E, cap_pad, F), BF16),
            pltpu.VMEM((E, 4, cap_pad, F), BF16),
            pltpu.VMEM((4, F, 2 * H), BF16),
            pltpu.VMEM((4, H, F), BF16),
            pltpu.VMEM((E, 4, cap_pad, H), BF16),
            pltpu.VMEM((E, cap_pad, F), BF16),
            pltpu.VMEM((E * cap_pad, F), BF16),
            pltpu.VMEM((T, E * cap_pad), BF16),
            pltpu.VMEM((1, T), F32),
            pltpu.VMEM((T, 128), F32),
            pltpu.VMEM((cap_pad, 2 * H), F32),
            dma((1,)), dma((9,)), dma((3,)), dma((3,)), dma((3,)), dma((3,)),
            dma((E,)), dma((E,)), dma((E,)), dma((E,)),
            dma((2, R)), dma((2, R)), dma((2, R)), dma((2, R)), dma((3, R)), dma((3, R)),
        ],
        compiler_params=pltpu.CompilerParams(
            collective_id=0, has_side_effects=True, vmem_limit_bytes=56 * 2**20
        ),
    )(tokens, route_ids.T, route_scores.T, *weights)
    placed = pl.pallas_call(
        place_kernel,
        out_shape=weight_shapes,
        in_specs=[pl.BlockSpec(memory_space=pltpu.SMEM)] + [hbm] * 6,
        out_specs=[hbm] * 3,
        scratch_shapes=[dma((3 * PIECES,))],
        compiler_params=pltpu.CompilerParams(has_side_effects=True, vmem_limit_bytes=56 * 2**20),
    )(partner, *weights, *swapped)
    return (summed, *placed)


def solution(mesh):
    return jax.shard_map(
        body,
        mesh=mesh,
        in_specs=(
            P("expert", "dp"),
            P("expert", None),
            P("expert", None),
            P(),
            P("expert", None, "dp"),
            P("expert", None, "dp"),
            P("expert", "dp", None),
        ),
        out_specs=(
            P("expert", "dp"),
            P("expert", None, "dp"),
            P("expert", None, "dp"),
            P("expert", "dp", None),
        ),
        check_vma=False,
    )
```

time: 171 us -> 487 us (2.85)
  Pallas kernels: 153 us -> 485 us
  other arithmetic: 10.8 us -> 0 us
    pallas_call x1 -> x2, Pallas kernels: 153 us -> 485 us  [the longest x1 336 us: body(): pl.pallas_call(place_kernel, out_shape=weight_shapes, in_specs=[pl.BlockS...]
    select_n x2 -> x0, other arithmetic: 10.8 us -> none  [the longest x1 6.36 us: body(): jnp.where(moved, sw_up, w_up)]
where the time goes in v2:
time: 487 us
  Pallas kernels  485 us (100%)
    pallas_call x1, Pallas kernels, body(): pl.pallas_call(place_kernel, out_shape=weight_shapes, in_specs=[pl.BlockS...  336 us
    pallas_call x1, Pallas kernels, body(): pl.pallas_call(functools.partial(kernel, E, cap_pad, R), out_shape=[jax.S...  149 us

profile of v2, /device:TPU:0, one launch (start us, length us, event | category | flops | bytes accessed | tf_op | source)
XLA Modules:
  0.0 486.6 jit_solution(5968633563494986891)
XLA Ops:
  0.6 149.4 %shard_map.102 = (bf16[320,1792]{1,0:T(8,128)(2,1)}, bf16[1,7168,256]{2,1,0:T(8,128)(2,1)}, bf16[1,7168,256]{2,1,0:T(8,128)(2,1)}, bf16[1,256,7168]{2,1,0:T(8,128)(2,1)}) custom-call(bf16[320,1792]{1,0:T(8,128)(2,1)} %tokens_hbm.1, s32[8,320]{1,0:T(8,128)} %bitcast.2, f32[8,320]{1,0:T(8,128)} %bitcast.3, bf16[1,7168,256]{2,1,0:T(8,128)(2,1)} %refs_0_.1, ...), custom_call_target="tpu_custom_call" | custom-call | tf_op jit(solution)/shard_map/pallas_call | solution.py:310
  150.0 0.0 copy-start
  150.0 335.6 %shard_map.103 = (bf16[1,7168,256]{2,1,0:T(8,128)(2,1)}, bf16[1,7168,256]{2,1,0:T(8,128)(2,1)}, bf16[1,256,7168]{2,1,0:T(8,128)(2,1)}) custom-call(s32[8]{0:T(128)} %partner.1, bf16[1,7168,256]{2,1,0:T(8,128)(2,1)} %refs_0_.1, bf16[1,7168,256]{2,1,0:T(8,128)(2,1)} %refs_1_.1, bf16[1,256,7168]{2,1,0:T(8,128)(2,1)} %refs_2_.1, ...), custom_call_target="tpu_custom_call" | custom-call | tf_op jit(solution)/shard_map/pallas_call | solution.py:336
  485.6 0.0 copy-done
  485.6 1.0 copy.12
Async XLA Ops:
  150.0 335.6 %copy-start = (bf16[320,1792]{1,0:T(8,128)(2,1)S(1)}, bf16[320,1792]{1,0:T(8,128)(2,1)}, u32[]{:S(2)}) copy-start(bf16[320,1792]{1,0:T(8,128)(2,1)} %get-tuple-element.22) | copy-start | bytes 3440644

commit v3 on v2

--- a/solution.py
+++ b/solution.py
@@ -64,14 +64,17 @@
         )
 
     def swap_copy(i):
-        src, dst = ((w_gate, sw_gate), (w_up, sw_up), (w_down, sw_down))[i]
-        return pltpu.make_async_remote_copy(
-            src, dst, swap_send.at[i], swap_recv.at[i],
+        src, dst = ((w_gate, sw_gate), (w_up, sw_up), (w_down, sw_down))[i // PIECES]
+        rows = src.shape[1] // PIECES
+        cut = (0, pl.ds(i % PIECES * rows, rows))
+        return pltpu.make_async_remote_copy(
+            src.at[cut], dst.at[cut], swap_send.at[i], swap_recv.at[i],
             device_id=(q, s + 1 - 2 * (s % 2)), device_id_type=MESH,
         )
 
     def peer_of(j):
-        return xor(s, (E - j) % E, E)
+        low = (E + 1 - j) // E
+        return xor(s, low * j + (1 - low) * (E + 1 - j), E)
 
     def z_copy(j):
         return pltpu.make_async_remote_copy(
@@ -119,6 +122,8 @@
     pl.semaphore_wait(barrier, E + 2)
     for i in range(3):
         wd_copy(i).start()
+    for i in range(3 * PIECES):
+        swap_copy(i).start()
 
     inside = ids[...] < E
     picks = jnp.sum(jnp.where(inside, ids[...], 0), axis=0, keepdims=True)
@@ -151,8 +156,6 @@
         a_copy(0, i).start()
     for c in own_copies:
         c.start()
-    for i in range(3):
-        swap_copy(i).start()
 
     gate_weight = 2.5 * jnp.sum(jnp.where(inside, scores[...], 0.0), axis=0, keepdims=True) / jnp.sum(
         scores[...], axis=0, keepdims=True
@@ -261,6 +264,7 @@
         mixed[:, n:n + 256] = (weight[:, :1] * dot(onehot_t[...], ret[:, n:n + 256])).astype(BF16)
     for i in range(3):
         wd_copy(i).wait_send()
+    for i in range(3 * PIECES):
         swap_copy(i).wait()
 
 
@@ -268,31 +272,47 @@
 
 
 def place_kernel(partner, *refs):
-    sources, targets, sem = (refs[0:3], refs[3:6]), refs[6:9], refs[9]
+    summed, own_set, other_set = refs[0], refs[1:4], refs[4:7]
+    mixed, targets = refs[7], refs[8:11]
+    rows_held, held, in_sem, out_sem = refs[11], refs[12:15], refs[15], refs[16]
     own = lax.axis_index("expert")
     moved = partner[own] != own
 
-    def pieces(group):
+    def loads(group):
         for i in range(3):
             rows = group[i].shape[1] // PIECES
             for n in range(PIECES):
                 cut = (0, pl.ds(n * rows, rows))
-                yield pltpu.make_async_copy(
-                    group[i].at[cut], targets[i].at[cut], sem.at[i * PIECES + n]
+                yield (
+                    pltpu.make_async_copy(
+                        group[i].at[cut], held[i].at[cut], in_sem.at[i * PIECES + n]
+                    ),
+                    pltpu.make_async_copy(
+                        held[i].at[cut], targets[i].at[cut], out_sem.at[i * PIECES + n]
+                    ),
                 )
 
     @pl.when(moved)
     def _():
-        for c in pieces(sources[1]):
-            c.start()
+        for load, _ in loads(other_set):
+            load.start()
 
     @pl.when(jnp.logical_not(moved))
     def _():
-        for c in pieces(sources[0]):
-            c.start()
-
-    for c in pieces(sources[0]):
-        c.wait()
+        for load, _ in loads(own_set):
+            load.start()
+
+    sum_load = pltpu.make_async_copy(summed, rows_held, in_sem.at[3 * PIECES])
+    sum_store = pltpu.make_async_copy(rows_held, mixed, out_sem.at[3 * PIECES])
+    sum_load.start()
+    for load, store in loads(own_set):
+        load.wait()
+        store.start()
+    sum_load.wait()
+    sum_store.start()
+    for _, store in loads(own_set):
+        store.wait()
+    sum_store.wait()
 
 
 def body(tokens, route_ids, route_scores, partner, w_gate, w_up, w_down):
@@ -325,7 +345,7 @@
             pltpu.VMEM((1, T), F32),
             pltpu.VMEM((T, 128), F32),
             pltpu.VMEM((cap_pad, 2 * H), F32),
-            dma((1,)), dma((9,)), dma((3,)), dma((3,)), dma((3,)), dma((3,)),
+            dma((1,)), dma((9,)), dma((3 * PIECES,)), dma((3 * PIECES,)), dma((3,)), dma((3,)),
             dma((E,)), dma((E,)), dma((E,)), dma((E,)),
             dma((2, R)), dma((2, R)), dma((2, R)), dma((2, R)), dma((3, R)), dma((3, R)),
         ],
@@ -333,15 +353,17 @@
             collective_id=0, has_side_effects=True, vmem_limit_bytes=56 * 2**20
         ),
     )(tokens, route_ids.T, route_scores.T, *weights)
-    placed = pl.pallas_call(
+    mixed_shape = jax.ShapeDtypeStruct((T, F), BF16)
+    return tuple(pl.pallas_call(
         place_kernel,
-        out_shape=weight_shapes,
-        in_specs=[pl.BlockSpec(memory_space=pltpu.SMEM)] + [hbm] * 6,
-        out_specs=[hbm] * 3,
-        scratch_shapes=[dma((3 * PIECES,))],
+        out_shape=[mixed_shape] + weight_shapes,
+        in_specs=[pl.BlockSpec(memory_space=pltpu.SMEM)] + [hbm] * 7,
+        out_specs=[hbm] * 4,
+        scratch_shapes=[pltpu.VMEM((T, F), BF16)]
+        + [pltpu.VMEM(w.shape, BF16) for w in weights]
+        + [dma((3 * PIECES + 1,)), dma((3 * PIECES + 1,))],
         compiler_params=pltpu.CompilerParams(has_side_effects=True, vmem_limit_bytes=56 * 2**20),
-    )(partner, *weights, *swapped)
-    return (summed, *placed)
+    )(partner, summed, *weights, *swapped))
 
 
 def solution(mesh):

time: 487 us -> 171 us (0.35)
  Pallas kernels: 485 us -> 170 us
    pallas_call x1, Pallas kernels: 336 us -> 9.94 us  [body(): pl.pallas_call(place_kernel, out_shape=[mixed_shape] + weight_shapes, in_...]
    pallas_call x1, Pallas kernels: 149 us -> 161 us  [body(): pl.pallas_call(functools.partial(kernel, E, cap_pad, R), out_shape=[jax.S...]
where the time goes in v3:
time: 171 us
  Pallas kernels  170 us (99%)
    pallas_call x1, Pallas kernels, body(): pl.pallas_call(functools.partial(kernel, E, cap_pad, R), out_shape=[jax.S...  161 us
    pallas_call x1, Pallas kernels, body(): pl.pallas_call(place_kernel, out_shape=[mixed_shape] + weight_shapes, in_...  9.94 us

profile of v3, /device:TPU:0, one launch (start us, length us, event | category | flops | bytes accessed | tf_op | source)
XLA Modules:
  0.0 171.1 jit_solution(7743297800023790577)
XLA Ops:
  0.6 160.5 %shard_map.102 = (bf16[320,1792]{1,0:T(8,128)(2,1)}, bf16[1,7168,256]{2,1,0:T(8,128)(2,1)}, bf16[1,7168,256]{2,1,0:T(8,128)(2,1)}, bf16[1,256,7168]{2,1,0:T(8,128)(2,1)}) custom-call(bf16[320,1792]{1,0:T(8,128)(2,1)} %tokens_hbm.1, s32[8,320]{1,0:T(8,128)} %bitcast.2, f32[8,320]{1,0:T(8,128)} %bitcast.3, bf16[1,7168,256]{2,1,0:T(8,128)(2,1)} %refs_1_.1, ...), custom_call_target="tpu_custom_call" | custom-call | tf_op jit(solution)/shard_map/pallas_call | solution.py:330
  161.2 9.9 %shard_map.103 = (bf16[320,1792]{1,0:T(8,128)(2,1)}, bf16[1,7168,256]{2,1,0:T(8,128)(2,1)}, bf16[1,7168,256]{2,1,0:T(8,128)(2,1)}, bf16[1,256,7168]{2,1,0:T(8,128)(2,1)}) custom-call(s32[8]{0:T(128)} %partner.1, bf16[320,1792]{1,0:T(8,128)(2,1)} %get-tuple-element.8.refs_0_, bf16[1,7168,256]{2,1,0:T(8,128)(2,1)} %refs_1_.1, bf16[1,7168,256]{2,1,0:T(8,128)(2,1)} %refs_2_.1, ...), custom_call_target="tpu_custom_call" | custom-call | tf_op jit(solution)/shard_map/pallas_call | solution.py:357
